TPU v7x, 1024 devices: a whole 4x4x32 slice. The times are simulated.
1024 devices in a mesh: freq: 64 (over z, core), srow: 4 (over y), rcol: 4 (over x).
Axes of the slice: x: 4, y: 4, z: 32, core: 2. Of those that a mesh axis runs over, the one named last changes fastest.
Arguments:
- data_time: bfloat16 [48, 2, 128, 128, 1024], P(('srow', 'rcol'), None, 'freq'), may hold values from -6 to 6
- block_cols: int32 [48, 2], P(('srow', 'rcol')), may hold values from 0 to 47, as said below
- row_counts: int32 [48], P(('srow', 'rcol')), may hold values from 1 to 2, as said below
Outputs:
- predicted: bfloat16 [64, 2, 48, 2, 128, 128], P('freq', None, ('srow', 'rcol'))
Inputs may be any that keep to these rules, and one draw needn't show every extreme that they name: Each block_cols[i, w] lies within 1 of i; the 2 entries of a row differ. Slots w < row_counts[i] of row i are live; the others are ignored.
All inputs are finite; a program needn't handle non-finite values.
Results may differ from a plain program's by a relative error of at most 0.0076.
Values may be sent and summed in bfloat16 or wider, within the bound.
A program may use at most 32 MiB of HBM per device.

v0:
```python
import math

import jax
import jax.numpy as jnp
from jax import lax
from jax.sharding import PartitionSpec as P


def shifted(value, axis, steps):
    count = lax.axis_size(axis)
    initial, last = (max(0, -steps), min(count, count - steps))
    return lax.ppermute(value, axis, [(source, source + steps) for source in range(initial, last)])


def spectral_table(samples, freq_count):
    time_index = jnp.arange(samples, dtype=jnp.int32)
    freq_bins = jnp.arange(freq_count, dtype=jnp.int32) + 1
    phase_int = time_index[:, None] * freq_bins[None, :] % samples
    angles = phase_int.astype(jnp.float32) * (2.0 * math.pi / samples)
    norm_factor = 1.0 / math.sqrt(samples)
    return (jnp.stack([jnp.cos(angles), -jnp.sin(angles)], axis=1) * norm_factor).astype(
        jnp.bfloat16
    )


def multiply(left_part, right_part):
    return jnp.einsum("rab,rbd->rad", left_part, right_part, preferred_element_type=jnp.float32)


def complex_product(left_band, extended, row_count, scale_factor):
    outputs = []
    for target in range(3):
        left_parts = []
        right_parts = []
        for source in range(3):
            inner_off = target - source + 1
            if 0 <= inner_off <= 2:
                left_parts.append(left_band[:, :, source])
                right_parts.append(extended[:, source : source + row_count, inner_off])
        left_all = jnp.concatenate(left_parts, axis=3)
        right_all = jnp.concatenate(right_parts, axis=2)
        real_part = multiply(left_all[0], right_all[0]) - multiply(left_all[1], right_all[1])
        imag_part = multiply(left_all[0], right_all[1]) + multiply(left_all[1], right_all[0])
        outputs.append(jnp.stack([real_part, imag_part]) * scale_factor)
    return jnp.stack(outputs, axis=2)


def border_rows(field):
    from_above = shifted(field[:, -1:], ("srow", "rcol"), 1)
    from_below = shifted(field[:, :1], ("srow", "rcol"), -1)
    return jnp.concatenate([from_above, field, from_below], axis=1)


def per_device(data_time, block_cols, row_counts):
    row_count = data_time.shape[0]
    slot_count = data_time.shape[1]
    block_width = data_time.shape[3]
    samples = data_time.shape[4]
    freq_count = lax.axis_size("freq")
    table = spectral_table(samples, freq_count)
    spectrum = jnp.einsum(
        "iwsrt,tcf->fciwsr", data_time, table, preferred_element_type=jnp.float32
    ).astype(jnp.bfloat16)
    arrived = lax.all_to_all(spectrum, "freq", split_axis=0, concat_axis=4, tiled=True)[0]
    first_row = lax.axis_index(("srow", "rcol")) * row_count
    row_index = first_row + jnp.arange(row_count, dtype=jnp.int32)
    offsets = block_cols - row_index[:, None] + 1
    live_slot = jnp.arange(slot_count, dtype=jnp.int32)[None, :] < row_counts[:, None]
    select = (
        (offsets[:, :, None] == jnp.arange(3, dtype=jnp.int32)[None, None, :])
        & live_slot[:, :, None]
    ).astype(jnp.bfloat16)
    band_rows = jnp.einsum(
        "iwo,ciwab->cioab", select, arrived, preferred_element_type=jnp.float32
    ).astype(jnp.bfloat16)
    scale_factor = (3.0 * block_width) ** (-0.5)
    first_order = complex_product(
        band_rows, border_rows(band_rows), row_count, scale_factor
    ).astype(jnp.bfloat16)
    second_order = complex_product(band_rows, border_rows(first_order), row_count, scale_factor)
    difference = first_order.astype(jnp.float32) - second_order
    result = jnp.einsum("iwo,cioab->ciwab", select.astype(jnp.float32), difference)
    return result.astype(jnp.bfloat16)[None]


def solution(mesh):
    return jax.shard_map(
        per_device,
        mesh=mesh,
        in_specs=(
            P(("srow", "rcol"), None, "freq", None, None),
            P(("srow", "rcol"), None),
            P(("srow", "rcol")),
        ),
        out_specs=P("freq", None, ("srow", "rcol"), None, None, None),
        check_vma=False,
    )
```

profile of v0, /device:TPU:6, one launch (start us, length us, event | category | flops | bytes accessed | tf_op | source)
XLA Modules:
  0.0 126.3 jit_solution(16398136257079791081)
XLA Ops:
  0.0 1.1 fusion.67
  1.1 0.8 copy-done
  1.9 1.2 fusion.11
  3.1 1.2 copy.126
  4.2 29.3 %all-to-all-start = ((bf16[64,2,3,2,2,128]{5,4,3,2,1,0:T(2,128)(2,1)}), bf16[64,2,3,2,2,128]{5,4,3,2,1,0:T(2,128)(2,1)S(1)}, u32[]{:S(2)}, u32[]{:S(2)}) async-start(bf16[64,2,3,2,2,128]{5,4,3,2,1,0:T(2,128)(2,1)} %copy.126), calls=%async_computation | async-start | bytes 786432 | tf_op jit(solution)/shard_map/all_to_all | solution.py:64
  33.8 53.6 %all-to-all-done = bf16[64,2,3,2,2,128]{5,4,3,2,1,0:T(2,128)(2,1)S(1)} async-done(((bf16[64,2,3,2,2,128]{5,4,3,2,1,0:T(2,128)(2,1)}), bf16[64,2,3,2,2,128]{5,4,3,2,1,0:T(2,128)(2,1)S(1)}, u32[]{:S(2)}, u32[]{:S(2)}) %all-to-all-start) | async-done | bytes 393248 | tf_op jit(solution)/shard_map/all_to_all | solution.py:64
  87.4 0.3 copy.127
  87.8 0.7 fusion.4
  88.7 3.4 %collective-permute-start = (bf16[2,1,3,128,128]{4,2,3,0,1:T(4,128)(2,1)S(1)}, bf16[2,1,3,128,128]{4,2,3,0,1:T(4,128)(2,1)S(1)}, u32[]{:S(2)}, u32[]{:S(2)}) collective-permute-start(bf16[2,1,3,128,128]{4,2,3,0,1:T(4,128)(2,1)S(1)} %get-tuple-element.18), channel_id=1, source_target_pairs={{0,1},{1,2},{2,3},{3,4},{4,5},{5,6},{6,7},{7,8},{8,9},{9,10},{10,1... | collective-permute-start | bytes 589832 | tf_op jit(solution)/shard_map/ppermute | solution.py:12
  92.1 2.4 %collective-permute-start.1 = (bf16[2,1,3,128,128]{4,2,3,0,1:T(4,128)(2,1)S(1)}, bf16[2,1,3,128,128]{4,2,3,0,1:T(4,128)(2,1)S(1)}, u32[]{:S(2)}, u32[]{:S(2)}) collective-permute-start(bf16[2,1,3,128,128]{4,2,3,0,1:T(4,128)(2,1)S(1)} %get-tuple-element.19), channel_id=1, source_target_pairs={{1,0},{2,1},{3,2},{4,3},{5,4},{6,5},{7,6},{8,7},{9,8},{10,9},{11,1... | collective-permute-start | bytes 589832 | tf_op jit(solution)/shard_map/ppermute | solution.py:12
  94.5 3.8 %collective-permute-done = bf16[2,1,3,128,128]{4,2,3,0,1:T(4,128)(2,1)S(1)} collective-permute-done((bf16[2,1,3,128,128]{4,2,3,0,1:T(4,128)(2,1)S(1)}, bf16[2,1,3,128,128]{4,2,3,0,1:T(4,128)(2,1)S(1)}, u32[]{:S(2)}, u32[]{:S(2)}) %collective-permute-start) | collective-permute-done | bytes 196640 | tf_op jit(solution)/shard_map/ppermute | solution.py:12
  98.4 5.2 %collective-permute-done.1 = bf16[2,1,3,128,128]{4,2,3,0,1:T(4,128)(2,1)S(1)} collective-permute-done((bf16[2,1,3,128,128]{4,2,3,0,1:T(4,128)(2,1)S(1)}, bf16[2,1,3,128,128]{4,2,3,0,1:T(4,128)(2,1)S(1)}, u32[]{:S(2)}, u32[]{:S(2)}) %collective-permute-start.1) | collective-permute-done | bytes 196640 | tf_op jit(solution)/shard_map/ppermute | solution.py:12
  103.6 3.2 %pad_maximum_fusion.7 = (bf16[2,3,1,128,128]{4,2,3,0,1:T(2,128)(2,1)S(1)}, bf16[2,3,1,128,128]{4,2,3,0,1:T(2,128)(2,1)S(1)}, bf16[2,3,1,128,128]{4,2,3,0,1:T(2,1...) fusion(bf16[2,3,3,128,128]{4,2,3,0,1:T(4,128)(2,1)S(1)} %fusion, ...), kind=kLoop, calls=%fused_computation.44 | loop fusion | flops 1572864 | bytes 3866624 | tf_op jit(solution)/shard_map/slice | solution.py:39
  107.1 0.2 fusion.68
  107.5 0.2 fusion.71
  108.1 0.2 fusion.44
  108.3 0.2 fusion.43
  108.6 0.2 fusion.27
  108.8 0.2 fusion.28
  109.0 0.2 fusion.23
  109.4 0.2 fusion.25
  109.6 0.2 fusion.26
  110.2 1.9 %collective-permute-start.2 = (bf16[2,1,3,128,128]{4,3,1,0,2:T(8,128)(2,1)S(1)}, bf16[2,1,3,128,128]{4,3,1,0,2:T(8,128)(2,1)S(1)}, u32[]{:S(2)}, u32[]{:S(2)}) collective-permute-start(bf16[2,1,3,128,128]{4,3,1,0,2:T(8,128)(2,1)S(1)} %get-tuple-element.22), channel_id=1, source_target_pairs={{0,1},{1,2},{2,3},{3,4},{4,5},{5,6},{6,7},{7,8},{8,9},{9,10},{10,1... | collective-permute-start | bytes 589832 | tf_op jit(solution)/shard_map/ppermute | solution.py:12
  112.1 3.9 %collective-permute-start.3 = (bf16[2,1,3,128,128]{4,3,1,0,2:T(8,128)(2,1)S(1)}, bf16[2,1,3,128,128]{4,3,1,0,2:T(8,128)(2,1)S(1)}, u32[]{:S(2)}, u32[]{:S(2)}) collective-permute-start(bf16[2,1,3,128,128]{4,3,1,0,2:T(8,128)(2,1)S(1)} %get-tuple-element.23), channel_id=1, source_target_pairs={{1,0},{2,1},{3,2},{4,3},{5,4},{6,5},{7,6},{8,7},{9,8},{10,9},{11,1... | collective-permute-start | bytes 589832 | tf_op jit(solution)/shard_map/ppermute | solution.py:12
  116.2 1.6 %collective-permute-done.2 = bf16[2,1,3,128,128]{4,3,1,0,2:T(8,128)(2,1)S(1)} collective-permute-done((bf16[2,1,3,128,128]{4,3,1,0,2:T(8,128)(2,1)S(1)}, bf16[2,1,3,128,128]{4,3,1,0,2:T(8,128)(2,1)S(1)}, u32[]{:S(2)}, u32[]{:S(2)}) %collective-permute-start.2) | collective-permute-done | bytes 196640 | tf_op jit(solution)/shard_map/ppermute | solution.py:12
  117.8 4.0 %collective-permute-done.3 = bf16[2,1,3,128,128]{4,3,1,0,2:T(8,128)(2,1)S(1)} collective-permute-done((bf16[2,1,3,128,128]{4,3,1,0,2:T(8,128)(2,1)S(1)}, bf16[2,1,3,128,128]{4,3,1,0,2:T(8,128)(2,1)S(1)}, u32[]{:S(2)}, u32[]{:S(2)}) %collective-permute-start.3) | collective-permute-done | bytes 196640 | tf_op jit(solution)/shard_map/ppermute | solution.py:12
  121.9 0.2 fusion.46
  122.2 0.2 fusion.45
  123.2 0.2 fusion.19
  123.5 0.2 fusion.20
  124.8 0.7 fusion.14
  125.5 0.8 copy.140
  (42 shorter events, 3.6 us)
Async XLA Ops:
  0.0 1.9 %copy-start = (bf16[3,2,2,128,1024]{4,3,2,1,0:T(8,128)(2,1)S(1)}, bf16[3,2,2,128,1024]{4,3,2,1,0:T(8,128)(2,1)}, u32[]{:S(2)}) copy-start(bf16[3,2,2,128,1024]{4,3,2,1,0:T(8,128)(2,1)} %param.3) | copy-start | bytes 9437188
  3.1 30.6 %copy-start.1 = (s32[3,2]{0,1:T(2,128)S(1)}, s32[3,2]{0,1:T(2,128)}, u32[]{:S(2)}) copy-start(s32[3,2]{0,1:T(2,128)} %param.4) | copy-start | bytes 76
  3.1 30.7 %copy-start.2 = (s32[3]{0:T(128)S(1)}, s32[3]{0:T(128)}, u32[]{:S(2)}) copy-start(s32[3]{0:T(128)} %param.5) | copy-start | bytes 40
  4.2 83.2 %all-to-all-start = ((bf16[64,2,3,2,2,128]{5,4,3,2,1,0:T(2,128)(2,1)}), bf16[64,2,3,2,2,128]{5,4,3,2,1,0:T(2,128)(2,1)S(1)}, u32[]{:S(2)}, u32[]{:S(2)}) async-start(bf16[64,2,3,2,2,128]{5,4,3,2,1,0:T(2,128)(2,1)} %copy.126), calls=%async_computation | async-start | bytes 786432 | tf_op jit(solution)/shard_map/all_to_all | solution.py:64
  88.7 9.7 %collective-permute-start = (bf16[2,1,3,128,128]{4,2,3,0,1:T(4,128)(2,1)S(1)}, bf16[2,1,3,128,128]{4,2,3,0,1:T(4,128)(2,1)S(1)}, u32[]{:S(2)}, u32[]{:S(2)}) collective-permute-start(bf16[2,1,3,128,128]{4,2,3,0,1:T(4,128)(2,1)S(1)} %get-tuple-element.18), channel_id=1, source_target_pairs={{0,1},{1,2},{2,3},{3,4},{4,5},{5,6},{6,7},{7,8},{8,9},{9,10},{10,1... | collective-permute-start | bytes 589832 | tf_op jit(solution)/shard_map/ppermute | solution.py:12
  92.1 11.5 %collective-permute-start.1 = (bf16[2,1,3,128,128]{4,2,3,0,1:T(4,128)(2,1)S(1)}, bf16[2,1,3,128,128]{4,2,3,0,1:T(4,128)(2,1)S(1)}, u32[]{:S(2)}, u32[]{:S(2)}) collective-permute-start(bf16[2,1,3,128,128]{4,2,3,0,1:T(4,128)(2,1)S(1)} %get-tuple-element.19), channel_id=1, source_target_pairs={{1,0},{2,1},{3,2},{4,3},{5,4},{6,5},{7,6},{8,7},{9,8},{10,9},{11,1... | collective-permute-start | bytes 589832 | tf_op jit(solution)/shard_map/ppermute | solution.py:12
  110.2 7.6 %collective-permute-start.2 = (bf16[2,1,3,128,128]{4,3,1,0,2:T(8,128)(2,1)S(1)}, bf16[2,1,3,128,128]{4,3,1,0,2:T(8,128)(2,1)S(1)}, u32[]{:S(2)}, u32[]{:S(2)}) collective-permute-start(bf16[2,1,3,128,128]{4,3,1,0,2:T(8,128)(2,1)S(1)} %get-tuple-element.22), channel_id=1, source_target_pairs={{0,1},{1,2},{2,3},{3,4},{4,5},{5,6},{6,7},{7,8},{8,9},{9,10},{10,1... | collective-permute-start | bytes 589832 | tf_op jit(solution)/shard_map/ppermute | solution.py:12
  112.1 9.7 %collective-permute-start.3 = (bf16[2,1,3,128,128]{4,3,1,0,2:T(8,128)(2,1)S(1)}, bf16[2,1,3,128,128]{4,3,1,0,2:T(8,128)(2,1)S(1)}, u32[]{:S(2)}, u32[]{:S(2)}) collective-permute-start(bf16[2,1,3,128,128]{4,3,1,0,2:T(8,128)(2,1)S(1)} %get-tuple-element.23), channel_id=1, source_target_pairs={{1,0},{2,1},{3,2},{4,3},{5,4},{6,5},{7,6},{8,7},{9,8},{10,9},{11,1... | collective-permute-start | bytes 589832 | tf_op jit(solution)/shard_map/ppermute | solution.py:12
where the time goes:
time: 127 us; the launch traced here: 126 us
  waiting for transfers between devices  68.3 us (54%)
  starting transfers between devices  41 us (32%)
  matrix products  7.59 us (6%)
  other arithmetic  5.34 us (4%)
  local copies, waits for them, and re-layouts  3.58 us (3%)
    all_to_all x1, waiting for transfers between devices, per_device(): lax.all_to_all(spectrum, 'freq', split_axis=0, concat_axis=4, tiled=True)[0]  53.6 us
    all_to_all x1, starting transfers between devices, per_device(): lax.all_to_all(spectrum, 'freq', split_axis=0, concat_axis=4, tiled=True)[0]  29.3 us
    ppermute x4, waiting for transfers between devices, shifted(): lax.ppermute(value, axis, [(source, source + steps) for source in range(i...  14.7 us
    ppermute x4, starting transfers between devices, shifted(): lax.ppermute(value, axis, [(source, source + steps) for source in range(i...  11.7 us
    dot_general x24, matrix products, multiply(): jnp.einsum('rab,rbd->rad', left_part, right_part, preferred_element_type=...  5.04 us
    slice x3, other arithmetic, complex_product(): right_parts.append(extended[:, source:source + row_count, inner_off])  3.34 us
  transfers between devices with their start and end apart: 5, of which 5 were waited for; matrix products, arithmetic and copies ran while one was open for 0% of the time, Pallas kernels for 0%

commit v1 on v0

v1 whole, which is shorter than its diff:
```python
import functools
import math

import jax
import jax.numpy as jnp
import numpy as np
from jax import lax
from jax.experimental import pallas as pl
from jax.experimental.pallas import tpu as pltpu
from jax.sharding import PartitionSpec as P

BS = 128
PAIR = 2 * BS
ROWS = 3
SLOTS = 2
GROUP = 8
MESH = pl.DeviceIdType.MESH


def spectral_table(samples, freq_count):
    time_index = np.arange(samples, dtype=np.int64)
    freq_bins = np.arange(freq_count, dtype=np.int64) + 1
    phase_int = freq_bins[:, None] * time_index[None, :] % samples
    angles = phase_int.astype(np.float32) * np.float32(2.0 * math.pi / samples)
    table = np.concatenate([np.cos(angles), -np.sin(angles)], axis=0)
    return (table * np.float32(1.0 / math.sqrt(samples))).astype(jnp.bfloat16)


def kernel(
    freqs, srows, rcols,
    x_hbm, table_hbm, meta_ref, out_ref,
    xv, tv, spread, sendbuf, recv, above, below, meta_up, meta_down, gather, bands, firsts,
    load_sem, table_sem, own_sem, send_sem, recv_sem, fsend_sem, frecv_sem, msend_sem, mrecv_sem,
):
    chips = freqs // 2
    me = lax.axis_index("freq")
    zpos, core = me // 2, me % 2
    grow = lax.axis_index("srow") * rcols + lax.axis_index("rcol")
    groups = srows * rcols
    nxt, prv = (grow + 1) % groups, (grow + groups - 1) % groups
    nxt_id = (me, nxt // rcols, nxt % rcols)
    prv_id = (me, prv // rcols, prv % rcols)
    pairs = ROWS * SLOTS

    table_copy = pltpu.make_async_copy(table_hbm, tv, table_sem)
    table_copy.start()
    loads = [pltpu.make_async_copy(x_hbm.at[n], xv.at[n], load_sem.at[n]) for n in range(pairs)]
    for load in loads:
        load.start()

    barrier = pltpu.get_barrier_semaphore()

    def greet(n, carry):
        pl.semaphore_signal(
            barrier, inc=1, device_id={"freq": (me + n) % freqs}, device_id_type=MESH
        )
        return carry

    lax.fori_loop(1, freqs, greet, 0)
    pl.semaphore_signal(barrier, inc=1, device_id=nxt_id, device_id_type=MESH)
    pl.semaphore_signal(barrier, inc=1, device_id=prv_id, device_id_type=MESH)

    table_copy.wait()
    for n in range(pairs):
        loads[n].wait()
        row, slot = n // SLOTS, n % SLOTS
        value = lax.dot_general(
            tv[...], xv[n], (((1,), (1,)), ((), ())), preferred_element_type=jnp.float32
        )
        for part in range(2):
            for trace in range(2):
                place = row * 8 + part * 4 + slot * 2 + trace
                spread[pl.ds(place, freqs, stride=ROWS * 8), :] = value[
                    part * freqs : (part + 1) * freqs, trace * BS : (trace + 1) * BS
                ]
    sendbuf[...] = spread[...].reshape(freqs, ROWS, 8, BS).astype(jnp.bfloat16)

    pl.semaphore_wait(barrier, freqs + 1)

    own_copy = pltpu.make_async_copy(
        sendbuf.at[me], recv.at[2 * (chips - 1) + core], own_sem
    )
    own_copy.start()

    def chip_of(step, sign):
        reach = chips // 2 - (step + 1) // 2
        way = 1 - 2 * ((step + 1) % 2)
        return (zpos + chips + sign * way * reach) % chips

    def send_to(step, other, target):
        return pltpu.make_async_remote_copy(
            src_ref=sendbuf.at[target],
            dst_ref=recv.at[2 * step + core],
            send_sem=send_sem,
            recv_sem=recv_sem.at[step // (GROUP // 2)],
            device_id={"freq": target},
            device_id_type=MESH,
        )

    def send(step, carry):
        chip = chip_of(step, 1)
        for other in range(2):
            send_to(step, other, 2 * chip + other).start()
        return carry

    lax.fori_loop(0, chips - 1, send, 0)
    send_to(chips - 1, 0, 2 * zpos + (1 - core)).start()

    def remote(src, dst, ssem, rsem, target):
        return pltpu.make_async_remote_copy(
            src_ref=src, dst_ref=dst, send_sem=ssem, recv_sem=rsem,
            device_id=target, device_id_type=MESH,
        )

    meta_copies = [
        remote(meta_ref, meta_up, msend_sem.at[0], mrecv_sem.at[0], nxt_id),
        remote(meta_ref, meta_down, msend_sem.at[1], mrecv_sem.at[1], prv_id),
    ]
    for copy in meta_copies:
        copy.start()

    arrival = lax.broadcasted_iota(jnp.int32, (1, 8 * freqs), 1)
    step = arrival >> 4
    reach = chips // 2 - ((step + 1) >> 1)
    way = 1 - 2 * ((step + 1) & 1)
    origin = ((zpos + chips - way * reach) & (chips - 1)) * 2 + ((arrival >> 3) & 1)
    key_in = origin * 8 + (arrival & 7)
    place = lax.broadcasted_iota(jnp.int32, (8 * freqs, 1), 0)
    trace_index = place & (BS - 1)
    key_out = (
        (trace_index >> 1) * 8
        + ((place >> 7) & 1) * 4
        + ((place >> 8) & 1) * 2
        + (trace_index & 1)
    )
    gather[...] = jnp.where(key_in == key_out, 1.0, 0.0).astype(jnp.bfloat16)

    batches = freqs // GROUP

    def border(first):
        span = pl.ds(first, GROUP)
        return (
            remote(recv.at[span, pl.ds(0, 2)], below.at[span], fsend_sem.at[0], frecv_sem.at[0], prv_id),
            remote(recv.at[span, pl.ds(1, 2)], above.at[span], fsend_sem.at[1], frecv_sem.at[1], nxt_id),
        )

    def relay(batch, carry):
        span = recv.at[pl.ds(batch * GROUP, GROUP)]
        remote(span, span, send_sem, recv_sem.at[batch], prv_id).wait_recv()
        for copy in border(batch * GROUP):
            copy.start()
        return carry

    lax.fori_loop(0, batches - 1, relay, 0)
    span = recv.at[pl.ds(0, GROUP - 1)]
    remote(span, span, send_sem, recv_sem.at[batches - 1], prv_id).wait_recv()
    own_copy.wait()
    for copy in border((batches - 1) * GROUP):
        copy.start()

    def rows_of(ref, index):
        return ref[:, index].astype(jnp.float32).reshape(8 * freqs, BS).astype(jnp.bfloat16)

    def place_band(row, block, offsets):
        for shift in range(3):
            parts = []
            for part in range(2):
                total = None
                for slot in range(SLOTS):
                    first = slot * PAIR + part * BS
                    live = jnp.where(offsets[slot] == float(shift), block[first : first + BS], 0.0)
                    total = live if total is None else total + live
                parts.append(total)
            bands[row, shift, :BS, :BS] = parts[0].astype(jnp.bfloat16)
            bands[row, shift, :BS, BS:] = parts[1].astype(jnp.bfloat16)
            bands[row, shift, BS:, :BS] = (-parts[1]).astype(jnp.bfloat16)
            bands[row, shift, BS:, BS:] = parts[0].astype(jnp.bfloat16)

    def assemble(ref, indices, rows, meta):
        stacked = [rows_of(ref, index) for index in indices]
        joined = stacked[0] if len(stacked) == 1 else jnp.concatenate(stacked, axis=1)
        blocks = jnp.dot(gather[...], joined, preferred_element_type=jnp.float32)
        for n, (index, row) in enumerate(zip(indices, rows)):
            offsets = [meta[2 * index + slot : 2 * index + slot + 1, :] for slot in range(SLOTS)]
            place_band(row, blocks[:, n * BS : (n + 1) * BS], offsets)

    scale = (3.0 * BS) ** (-0.5)

    def product(row, target, right, shift_row):
        total = None
        for source in range(3):
            inner = target - source + 1
            if 0 <= inner <= 2:
                term = jnp.dot(
                    bands[row, source, :BS, :],
                    right[row + source - 1 - shift_row, inner],
                    preferred_element_type=jnp.float32,
                )
                total = term if total is None else total + term
        return total * scale

    def first_row(row):
        for target in range(3):
            value = product(row, target, bands, 0).astype(jnp.bfloat16)
            firsts[row - 1, target, :BS, :] = value
            firsts[row - 1, target, BS:, :BS] = -value[:, BS:]
            firsts[row - 1, target, BS:, BS:] = value[:, :BS]

    assemble(recv, [0, 1], [2, 3], meta_ref)
    assemble(recv, [2], [4], meta_ref)
    first_row(3)

    whole_above = remote(above, above, fsend_sem.at[1], frecv_sem.at[1], nxt_id)
    whole_below = remote(below, below, fsend_sem.at[0], frecv_sem.at[0], prv_id)
    for copy in meta_copies:
        copy.wait_recv()
    whole_above.wait_recv()
    assemble(above, [0, 1], [0, 1], meta_up[2:6, :])
    first_row(1)
    first_row(2)
    whole_below.wait_recv()
    assemble(below, [0, 1], [5, 6], meta_down)
    first_row(4)
    first_row(5)

    for index in range(ROWS):
        row = index + 2
        results = []
        for target in range(3):
            second = product(row, target, firsts, 1)
            results.append(firsts[row - 1, target, :BS, :].astype(jnp.float32) - second)
        for slot in range(SLOTS):
            offset = meta_ref[2 * index + slot : 2 * index + slot + 1, :]
            for part in range(2):
                total = None
                for target in range(3):
                    term = jnp.where(
                        offset == float(target), results[target][:, part * BS : (part + 1) * BS], 0.0
                    )
                    total = term if total is None else total + term
                out_ref[0, part, index, slot] = total.astype(jnp.bfloat16)

    sent = recv.at[pl.ds(0, freqs - 1)]
    remote(sent, sent, send_sem, recv_sem.at[0], prv_id).wait_send()
    whole_above.wait_send()
    whole_below.wait_send()
    for copy in meta_copies:
        copy.wait_send()


def solution(mesh):
    freqs, srows, rcols = mesh.shape["freq"], mesh.shape["srow"], mesh.shape["rcol"]

    def per_device(data_time, block_cols, row_counts):
        samples = data_time.shape[-1]
        pairs = ROWS * SLOTS
        first_row = lax.axis_index(("srow", "rcol")) * ROWS
        row_index = first_row + jnp.arange(ROWS, dtype=jnp.int32)
        live = jnp.arange(SLOTS, dtype=jnp.int32)[None, :] < row_counts[:, None]
        offsets = jnp.where(live, block_cols - row_index[:, None] + 1, -1)
        meta = jnp.broadcast_to(offsets.astype(jnp.float32).reshape(pairs, 1), (pairs, BS))
        meta = jnp.concatenate([meta, jnp.full((8 - pairs, BS), -1.0, jnp.float32)], axis=0)
        table = jnp.asarray(spectral_table(samples, freqs))
        return pl.pallas_call(
            functools.partial(kernel, freqs, srows, rcols),
            out_shape=jax.ShapeDtypeStruct((1, 2, ROWS, SLOTS, BS, BS), jnp.bfloat16),
            in_specs=[
                pl.BlockSpec(memory_space=pl.ANY),
                pl.BlockSpec(memory_space=pl.ANY),
                pl.BlockSpec(memory_space=pltpu.VMEM),
            ],
            out_specs=pl.BlockSpec(memory_space=pltpu.VMEM),
            scratch_shapes=[
                pltpu.VMEM((pairs, PAIR, samples), jnp.bfloat16),
                pltpu.VMEM((2 * freqs, samples), jnp.bfloat16),
                pltpu.VMEM((freqs * ROWS * 8, BS), jnp.float32),
                pltpu.VMEM((freqs, ROWS, 8, BS), jnp.bfloat16),
                pltpu.VMEM((freqs, ROWS, 8, BS), jnp.bfloat16),
                pltpu.VMEM((freqs, 2, 8, BS), jnp.bfloat16),
                pltpu.VMEM((freqs, 2, 8, BS), jnp.bfloat16),
                pltpu.VMEM((8, BS), jnp.float32),
                pltpu.VMEM((8, BS), jnp.float32),
                pltpu.VMEM((8 * freqs, 8 * freqs), jnp.bfloat16),
                pltpu.VMEM((7, 3, PAIR, PAIR), jnp.bfloat16),
                pltpu.VMEM((5, 3, PAIR, PAIR), jnp.bfloat16),
                pltpu.SemaphoreType.DMA((pairs,)),
                pltpu.SemaphoreType.DMA,
                pltpu.SemaphoreType.DMA,
                pltpu.SemaphoreType.DMA,
                pltpu.SemaphoreType.DMA((freqs // GROUP,)),
                pltpu.SemaphoreType.DMA((2,)),
                pltpu.SemaphoreType.DMA((2,)),
                pltpu.SemaphoreType.DMA((2,)),
                pltpu.SemaphoreType.DMA((2,)),
            ],
            compiler_params=pltpu.CompilerParams(
                collective_id=0, has_side_effects=True, vmem_limit_bytes=40 * 1024 * 1024
            ),
        )(data_time.reshape(pairs, PAIR, samples), table, meta)

    return jax.shard_map(
        per_device,
        mesh=mesh,
        in_specs=(
            P(("srow", "rcol"), None, "freq", None, None),
            P(("srow", "rcol"), None),
            P(("srow", "rcol")),
        ),
        out_specs=P("freq", None, ("srow", "rcol"), None, None, None),
        check_vma=False,
    )
```

time: 127 us -> 80.6 us (0.63)
  the two profiles are of different devices: /device:TPU:6 before, /device:TPU:1 now
where the time goes in v1:
time: 80.6 us; the launch traced here: 80.4 us
  Pallas kernels  75.8 us (94%)
  local copies, waits for them, and re-layouts  3.85 us (5%)
    pallas_call x1, Pallas kernels, per_device(): pl.pallas_call(functools.partial(kernel, freqs, srows, rcols), out_shape=...  75.8 us
    unnamed x5, local copies, waits for them, and re-layouts  3.59 us

profile of v1, /device:TPU:1, one launch (start us, length us, event | category | flops | bytes accessed | tf_op | source)
XLA Modules:
  0.0 80.4 jit_solution(3732093869662754761)
XLA Ops:
  0.0 0.7 fusion
  0.7 0.1 copy.6
  0.8 0.1 broadcast_in_dim.7
  0.9 0.1 concatenate.6.meta_ref
  1.0 0.0 copy-start
  1.0 1.9 %copy-done = bf16[3,2,2,128,1024]{4,3,2,1,0:T(8,128)(2,1)S(1)} copy-done((bf16[3,2,2,128,1024]{4,3,2,1,0:T(8,128)(2,1)S(1)}, bf16[3,2,2,128,1024]{4,3,2,1,0:T(8,128)(2,1)}, u32[]{:S(2)}) %copy-start) | copy-done | bytes 3145752
  2.8 0.0 copy-start.1
  2.8 0.9 %copy-done.1 = bf16[128,1024]{1,0:T(8,128)(2,1)S(1)} copy-done((bf16[128,1024]{1,0:T(8,128)(2,1)S(1)}, bf16[128,1024]{1,0:T(8,128)(2,1)}, u32[]{:S(2)}) %copy-start.1) | copy-done | bytes 262168
  3.8 75.8 %shard_map.46 = bf16[1,2,3,2,128,128]{5,4,3,2,1,0:T(8,128)(2,1)S(1)} custom-call(bf16[6,256,1024]{2,1,0:T(8,128)(2,1)S(1)} %bitcast.1, bf16[128,1024]{1,0:T(8,128)(2,1)S(1)} %copy-done.1, f32[8,128]{1,0:T(8,128)S(1)} %concatenate.6.meta_ref), custom_call_target="tpu_custom_call" | custom-call | tf_op jit(solution)/shard_map/pallas_call | solution.py:264
  79.6 0.7 copy.8
  (2 shorter events, 0.0 us)
Async XLA Ops:
  1.0 1.9 %copy-start = (bf16[3,2,2,128,1024]{4,3,2,1,0:T(8,128)(2,1)S(1)}, bf16[3,2,2,128,1024]{4,3,2,1,0:T(8,128)(2,1)}, u32[]{:S(2)}) copy-start(bf16[3,2,2,128,1024]{4,3,2,1,0:T(8,128)(2,1)} %param.4) | copy-start | bytes 9437188
  2.8 0.9 %copy-start.1 = (bf16[128,1024]{1,0:T(8,128)(2,1)S(1)}, bf16[128,1024]{1,0:T(8,128)(2,1)}, u32[]{:S(2)}) copy-start(bf16[128,1024]{1,0:T(8,128)(2,1)} %constant.19.clone.table_hbm) | copy-start | bytes 786436

commit v2 on v1

--- a/solution.py
+++ b/solution.py
@@ -13,7 +13,6 @@
 PAIR = 2 * BS
 ROWS = 3
 SLOTS = 2
-GROUP = 8
 MESH = pl.DeviceIdType.MESH
 
 
@@ -27,10 +26,10 @@
 
 
 def kernel(
-    freqs, srows, rcols,
-    x_hbm, table_hbm, meta_ref, out_ref,
-    xv, tv, spread, sendbuf, recv, above, below, meta_up, meta_down, gather, bands, firsts,
-    load_sem, table_sem, own_sem, send_sem, recv_sem, fsend_sem, frecv_sem, msend_sem, mrecv_sem,
+    freqs, srows, rcols, order, batches, plan,
+    x_hbm, table_hbm, cols_hbm, counts_hbm, out_ref,
+    xv, tv, cols_ref, counts_ref, meta_ref, spread, sendbuf, recv, above, below, meta_up, meta_down, gather, bands, firsts,
+    load_sem, table_sem, index_sem, own_sem, ready_sem, send_sem, recv_sem, fsend_sem, frecv_sem, msend_sem, mrecv_sem,
 ):
     chips = freqs // 2
     me = lax.axis_index("freq")
@@ -48,15 +47,26 @@
     for load in loads:
         load.start()
 
+    index_copies = [
+        pltpu.make_async_copy(cols_hbm, cols_ref, index_sem.at[0]),
+        pltpu.make_async_copy(counts_hbm, counts_ref, index_sem.at[1]),
+    ]
+    for copy in index_copies:
+        copy.start()
+
+    near = chips // 4
     barrier = pltpu.get_barrier_semaphore()
-
-    def greet(n, carry):
-        pl.semaphore_signal(
-            barrier, inc=1, device_id={"freq": (me + n) % freqs}, device_id_type=MESH
-        )
-        return carry
-
-    lax.fori_loop(1, freqs, greet, 0)
+    for reach in range(near, -1, -1):
+        for way in (1, -1):
+            chip = (zpos + chips + way * reach) % chips
+            for other in range(2):
+                if reach or (way, other) == (1, 0):
+                    pl.semaphore_signal(
+                        barrier,
+                        inc=1,
+                        device_id={"freq": 2 * chip + (other if reach else 1 - core)},
+                        device_id_type=MESH,
+                    )
     pl.semaphore_signal(barrier, inc=1, device_id=nxt_id, device_id_type=MESH)
     pl.semaphore_signal(barrier, inc=1, device_id=prv_id, device_id_type=MESH)
 
@@ -75,36 +85,16 @@
                 ]
     sendbuf[...] = spread[...].reshape(freqs, ROWS, 8, BS).astype(jnp.bfloat16)
 
-    pl.semaphore_wait(barrier, freqs + 1)
-
-    own_copy = pltpu.make_async_copy(
-        sendbuf.at[me], recv.at[2 * (chips - 1) + core], own_sem
-    )
-    own_copy.start()
-
-    def chip_of(step, sign):
-        reach = chips // 2 - (step + 1) // 2
-        way = 1 - 2 * ((step + 1) % 2)
-        return (zpos + chips + sign * way * reach) % chips
-
-    def send_to(step, other, target):
-        return pltpu.make_async_remote_copy(
-            src_ref=sendbuf.at[target],
-            dst_ref=recv.at[2 * step + core],
-            send_sem=send_sem,
-            recv_sem=recv_sem.at[step // (GROUP // 2)],
-            device_id={"freq": target},
-            device_id_type=MESH,
-        )
-
-    def send(step, carry):
-        chip = chip_of(step, 1)
-        for other in range(2):
-            send_to(step, other, 2 * chip + other).start()
-        return carry
-
-    lax.fori_loop(0, chips - 1, send, 0)
-    send_to(chips - 1, 0, 2 * zpos + (1 - core)).start()
+    for copy in index_copies:
+        copy.wait()
+    for row in range(ROWS):
+        for slot in range(SLOTS):
+            offset = cols_ref[slot : slot + 1, row : row + 1] - (ROWS * grow + row) + 1
+            offset = jnp.where(counts_ref[:, row : row + 1] > slot, offset, -1)
+            meta_ref[2 * row + slot : 2 * row + slot + 1, :] = jnp.broadcast_to(
+                offset.astype(jnp.float32), (1, BS)
+            )
+    meta_ref[pairs:, :] = jnp.full((8 - pairs, BS), -1.0, jnp.float32)
 
     def remote(src, dst, ssem, rsem, target):
         return pltpu.make_async_remote_copy(
@@ -112,18 +102,22 @@
             device_id=target, device_id_type=MESH,
         )
 
-    meta_copies = [
-        remote(meta_ref, meta_up, msend_sem.at[0], mrecv_sem.at[0], nxt_id),
-        remote(meta_ref, meta_down, msend_sem.at[1], mrecv_sem.at[1], prv_id),
-    ]
-    for copy in meta_copies:
-        copy.start()
+    def send(place):
+        chip = (zpos + chips + order[place]) % chips
+        batch = [low <= place < high for low, high in batches].index(True)
+        for other in range(2):
+            target = 2 * chip + (other if order[place] else 1 - core)
+            if order[place] or other == 0:
+                remote(
+                    sendbuf.at[target], recv.at[2 * place + core], send_sem, recv_sem.at[batch],
+                    {"freq": target},
+                ).start()
 
     arrival = lax.broadcasted_iota(jnp.int32, (1, 8 * freqs), 1)
-    step = arrival >> 4
-    reach = chips // 2 - ((step + 1) >> 1)
-    way = 1 - 2 * ((step + 1) & 1)
-    origin = ((zpos + chips - way * reach) & (chips - 1)) * 2 + ((arrival >> 3) & 1)
+    came = jnp.zeros_like(arrival)
+    for place, chip in enumerate(order):
+        came = jnp.where(arrival >> 4 == place, chip, came)
+    origin = ((zpos + chips - came) & (chips - 1)) * 2 + ((arrival >> 3) & 1)
     key_in = origin * 8 + (arrival & 7)
     place = lax.broadcasted_iota(jnp.int32, (8 * freqs, 1), 0)
     trace_index = place & (BS - 1)
@@ -135,28 +129,47 @@
     )
     gather[...] = jnp.where(key_in == key_out, 1.0, 0.0).astype(jnp.bfloat16)
 
-    batches = freqs // GROUP
-
-    def border(first):
-        span = pl.ds(first, GROUP)
-        return (
-            remote(recv.at[span, pl.ds(0, 2)], below.at[span], fsend_sem.at[0], frecv_sem.at[0], prv_id),
-            remote(recv.at[span, pl.ds(1, 2)], above.at[span], fsend_sem.at[1], frecv_sem.at[1], nxt_id),
+    def relay(batch):
+        low, high = batches[batch]
+        mine = low <= home < high
+        low, high = 2 * low, 2 * high
+        arrived = recv.at[pl.ds(low, high - low - mine)]
+        remote(arrived, arrived, send_sem, recv_sem.at[batch], prv_id).wait_recv()
+        if mine:
+            own_copy.wait()
+        span = pl.ds(low, high - low)
+        remote(
+            recv.at[span, pl.ds(0, 2)], below.at[span], fsend_sem.at[0], frecv_sem.at[0], prv_id
+        ).start()
+        remote(
+            recv.at[span, pl.ds(1, 2)], above.at[span], fsend_sem.at[1], frecv_sem.at[1], nxt_id
+        ).start()
+
+    pl.semaphore_wait(barrier, 4 * near + 3)
+    home = order.index(0)
+    own_copy = pltpu.make_async_copy(sendbuf.at[me], recv.at[2 * home + core], own_sem)
+    own_copy.start()
+    for way in (1, chips - 1):
+        pl.semaphore_signal(
+            ready_sem,
+            inc=1,
+            device_id={"freq": 2 * ((zpos + way * near) % chips) + core},
+            device_id_type=MESH,
         )
-
-    def relay(batch, carry):
-        span = recv.at[pl.ds(batch * GROUP, GROUP)]
-        remote(span, span, send_sem, recv_sem.at[batch], prv_id).wait_recv()
-        for copy in border(batch * GROUP):
-            copy.start()
-        return carry
-
-    lax.fori_loop(0, batches - 1, relay, 0)
-    span = recv.at[pl.ds(0, GROUP - 1)]
-    remote(span, span, send_sem, recv_sem.at[batches - 1], prv_id).wait_recv()
-    own_copy.wait()
-    for copy in border((batches - 1) * GROUP):
+    meta_copies = [
+        remote(meta_ref, meta_up, msend_sem.at[0], mrecv_sem.at[0], nxt_id),
+        remote(meta_ref, meta_down, msend_sem.at[1], mrecv_sem.at[1], prv_id),
+    ]
+    for copy in meta_copies:
         copy.start()
+    for kind, value in plan:
+        if kind == "send":
+            for place in range(*batches[value]):
+                send(place)
+        elif kind == "relay":
+            relay(value)
+        else:
+            pl.semaphore_wait(ready_sem, 2)
 
     def rows_of(ref, index):
         return ref[:, index].astype(jnp.float32).reshape(8 * freqs, BS).astype(jnp.bfloat16)
@@ -248,31 +261,53 @@
         copy.wait_send()
 
 
+def schedule(chips):
+    def both(*reaches):
+        return [step for reach in reaches for step in (reach, -reach)]
+
+    groups = [
+        both(8, 7, 6),
+        both(5, 4) + [0],
+        [16] + both(15, 14),
+        both(13, 12, 11),
+        both(10, 9),
+        both(3, 2, 1),
+    ]
+    order = [step for group in groups for step in group]
+    cuts = [sum(len(group) for group in groups[:n]) for n in range(len(groups) + 1)]
+    batches = list(zip(cuts[:-1], cuts[1:]))
+    plan = [
+        ("send", 0), ("send", 1), ("ready", 0), ("send", 2), ("send", 3), ("relay", 0), ("relay", 1),
+        ("send", 4), ("relay", 2), ("send", 5), ("relay", 3), ("relay", 4), ("relay", 5),
+    ]
+    return order, batches, plan
+
+
 def solution(mesh):
     freqs, srows, rcols = mesh.shape["freq"], mesh.shape["srow"], mesh.shape["rcol"]
 
     def per_device(data_time, block_cols, row_counts):
         samples = data_time.shape[-1]
         pairs = ROWS * SLOTS
-        first_row = lax.axis_index(("srow", "rcol")) * ROWS
-        row_index = first_row + jnp.arange(ROWS, dtype=jnp.int32)
-        live = jnp.arange(SLOTS, dtype=jnp.int32)[None, :] < row_counts[:, None]
-        offsets = jnp.where(live, block_cols - row_index[:, None] + 1, -1)
-        meta = jnp.broadcast_to(offsets.astype(jnp.float32).reshape(pairs, 1), (pairs, BS))
-        meta = jnp.concatenate([meta, jnp.full((8 - pairs, BS), -1.0, jnp.float32)], axis=0)
+        chips = freqs // 2
+        order, batches, plan = schedule(chips)
         table = jnp.asarray(spectral_table(samples, freqs))
         return pl.pallas_call(
-            functools.partial(kernel, freqs, srows, rcols),
+            functools.partial(kernel, freqs, srows, rcols, order, batches, plan),
             out_shape=jax.ShapeDtypeStruct((1, 2, ROWS, SLOTS, BS, BS), jnp.bfloat16),
             in_specs=[
                 pl.BlockSpec(memory_space=pl.ANY),
                 pl.BlockSpec(memory_space=pl.ANY),
-                pl.BlockSpec(memory_space=pltpu.VMEM),
+                pl.BlockSpec(memory_space=pl.ANY),
+                pl.BlockSpec(memory_space=pl.ANY),
             ],
             out_specs=pl.BlockSpec(memory_space=pltpu.VMEM),
             scratch_shapes=[
                 pltpu.VMEM((pairs, PAIR, samples), jnp.bfloat16),
                 pltpu.VMEM((2 * freqs, samples), jnp.bfloat16),
+                pltpu.VMEM((SLOTS, ROWS), jnp.int32),
+                pltpu.VMEM((1, ROWS), jnp.int32),
+                pltpu.VMEM((8, BS), jnp.float32),
                 pltpu.VMEM((freqs * ROWS * 8, BS), jnp.float32),
                 pltpu.VMEM((freqs, ROWS, 8, BS), jnp.bfloat16),
                 pltpu.VMEM((freqs, ROWS, 8, BS), jnp.bfloat16),
@@ -285,18 +320,25 @@
                 pltpu.VMEM((5, 3, PAIR, PAIR), jnp.bfloat16),
                 pltpu.SemaphoreType.DMA((pairs,)),
                 pltpu.SemaphoreType.DMA,
+                pltpu.SemaphoreType.DMA((2,)),
                 pltpu.SemaphoreType.DMA,
+                pltpu.SemaphoreType.REGULAR,
                 pltpu.SemaphoreType.DMA,
-                pltpu.SemaphoreType.DMA((freqs // GROUP,)),
+                pltpu.SemaphoreType.DMA((len(batches),)),
                 pltpu.SemaphoreType.DMA((2,)),
                 pltpu.SemaphoreType.DMA((2,)),
                 pltpu.SemaphoreType.DMA((2,)),
                 pltpu.SemaphoreType.DMA((2,)),
             ],
             compiler_params=pltpu.CompilerParams(
-                collective_id=0, has_side_effects=True, vmem_limit_bytes=40 * 1024 * 1024
+                collective_id=0, has_side_effects=True, vmem_limit_bytes=60 * 1024 * 1024
             ),
-        )(data_time.reshape(pairs, PAIR, samples), table, meta)
+        )(
+            data_time.reshape(pairs, PAIR, samples),
+            table,
+            block_cols.T,
+            row_counts.reshape(1, ROWS),
+        )
 
     return jax.shard_map(
         per_device,

time: 80.6 us -> 74.6 us (0.926)
  Pallas kernels: 75.8 us -> 72.7 us
  local copies, waits for them, and re-layouts: 3.85 us -> 1.77 us
    pallas_call x1, Pallas kernels: 75.8 us -> 72.7 us  [per_device(): pl.pallas_call(functools.partial(kernel, freqs, srows, rcols, order, batc...]
    unnamed x5 -> x1, local copies, waits for them, and re-layouts: 3.59 us -> 1.77 us
where the time goes in v2:
time: 74.6 us; the launch traced here: 74.4 us
  Pallas kernels  72.7 us (97%)
  local copies, waits for them, and re-layouts  1.77 us (2%)
    pallas_call x1, Pallas kernels, per_device(): pl.pallas_call(functools.partial(kernel, freqs, srows, rcols, order, batc...  72.7 us
    unnamed x1, local copies, waits for them, and re-layouts  1.77 us

profile of v2, /device:TPU:1, one launch (start us, length us, event | category | flops | bytes accessed | tf_op | source)
XLA Modules:
  0.0 74.4 jit_solution(13532841421380943549)
XLA Ops:
  0.0 72.7 %shard_map.46 = bf16[1,2,3,2,128,128]{5,4,3,2,1,0:T(8,128)(2,1)} custom-call(bf16[6,256,1024]{2,1,0:T(8,128)(2,1)} %bitcast.3, bf16[128,1024]{1,0:T(8,128)(2,1)} %constant.2.clone.table_hbm, s32[2,3]{1,0:T(2,128)} %bitcast.4, s32[1,3]{1,0:T(1,128)} %bitcast.5), custom_call_target="tpu_custom_call" | custom-call | tf_op jit(solution)/shard_map/pallas_call | solution.py:295
  72.7 1.8 %copy.6 = bf16[1,2,3,2,128,128]{5,4,3,2,1,0:T(8,128)(2,1)} copy(bf16[1,2,3,2,128,128]{5,4,3,2,1,0:T(8,128)(2,1)} %shard_map.46) | data formatting | bytes 786432

commit v3 on v2

v3 whole, which is shorter than its diff:
```python
import functools
import math

import jax
import jax.numpy as jnp
from jax import lax
from jax.experimental import pallas as pl
from jax.experimental.pallas import tpu as pltpu
from jax.sharding import PartitionSpec as P

BS = 128
PAIR = 2 * BS
ROWS = 3
SLOTS = 2
MESH = pl.DeviceIdType.MESH


def spectral_table(samples, freqs):
    row = lax.broadcasted_iota(jnp.int32, (2 * freqs, samples), 0)
    time = lax.broadcasted_iota(jnp.int32, (2 * freqs, samples), 1)
    part = (row >= freqs).astype(jnp.int32)
    phase = ((row - part * freqs + 1) * time + part * (samples // 4)) & (samples - 1)
    folded = jnp.abs(phase - samples // 2) - samples // 4
    angle = folded.astype(jnp.float32) * (2.0 * math.pi / samples)
    square = angle * angle
    value = jnp.full_like(square, -1.0 / math.factorial(11))
    for power in (9, 7, 5, 3, 1):
        value = value * square + (-1.0) ** (power // 2) / math.factorial(power)
    return (value * angle * (1.0 / math.sqrt(samples))).astype(jnp.bfloat16)


def kernel(
    freqs, srows, rcols, order, batches, plan, hops,
    x_hbm, cols_ref, out_ref,
    xv, tv, meta_ref, spread, sendbuf, recv, border, border_meta, gather, bands, firsts, partial, seconds,
    load_sem, own_sem, ready_sem, send_sem, recv_sem, fsend_sem, frecv_sem, msend_sem, mrecv_sem,
):
    chips = freqs // 2
    me = lax.axis_index("freq")
    zpos, core = me // 2, me % 2
    grow = lax.axis_index("srow") * rcols + lax.axis_index("rcol")
    groups = srows * rcols
    nxt, prv = (grow + 1) % groups, (grow + groups - 1) % groups
    has_nxt, has_prv = grow < groups - 1, grow > 0
    nxt_id = (me, nxt // rcols, nxt % rcols)
    prv_id = (me, prv // rcols, prv % rcols)
    pairs = ROWS * SLOTS
    home = order.index(0)

    loads = [pltpu.make_async_copy(x_hbm.at[n], xv.at[n], load_sem.at[n]) for n in range(pairs)]
    for load in loads:
        load.start()

    near, further = hops
    barrier = pltpu.get_barrier_semaphore()
    for reach in range(near, -1, -1):
        for way in (1, -1):
            chip = (zpos + chips + way * reach) % chips
            for other in range(2):
                if reach or (way, other) == (1, 0):
                    pl.semaphore_signal(
                        barrier,
                        inc=1,
                        device_id={"freq": 2 * chip + (other if reach else 1 - core)},
                        device_id_type=MESH,
                    )
    pl.semaphore_signal(barrier, inc=1, device_id=nxt_id, device_id_type=MESH)
    pl.semaphore_signal(barrier, inc=1, device_id=prv_id, device_id_type=MESH)

    tv[...] = spectral_table(tv.shape[1], freqs)
    for n in range(pairs):
        loads[n].wait()
        row, slot = n // SLOTS, n % SLOTS
        value = lax.dot_general(
            tv[...], xv[n], (((1,), (1,)), ((), ())), preferred_element_type=jnp.float32
        )
        for part in range(2):
            for trace in range(2):
                place = row * 8 + part * 4 + slot * 2 + trace
                spread[pl.ds(place, freqs, stride=ROWS * 8), :] = value[
                    part * freqs : (part + 1) * freqs, trace * BS : (trace + 1) * BS
                ]
    sendbuf[...] = spread[: freqs * ROWS * 8, :].reshape(freqs, ROWS, 8, BS).astype(jnp.bfloat16)

    for row in range(ROWS):
        for slot in range(SLOTS):
            offset = cols_ref[slot : slot + 1, row : row + 1] - (ROWS * grow + row) + 1
            meta_ref[2 * row + slot : 2 * row + slot + 1, :] = jnp.broadcast_to(
                offset.astype(jnp.float32), (1, BS)
            )
    meta_ref[pairs:, :] = jnp.full((8 - pairs, BS), -1.0, jnp.float32)

    def remote(src, dst, ssem, rsem, target):
        return pltpu.make_async_remote_copy(
            src_ref=src, dst_ref=dst, send_sem=ssem, recv_sem=rsem,
            device_id=target, device_id_type=MESH,
        )

    def send(place):
        chip = (zpos + chips + order[place]) % chips
        batch = [low <= place < high for low, high in batches].index(True)
        for other in range(2):
            target = 2 * chip + (other if order[place] else 1 - core)
            if order[place] or other == 0:
                remote(
                    sendbuf.at[target], recv.at[2 * place + core], send_sem.at[batch], recv_sem.at[batch],
                    {"freq": target},
                ).start()

    arrival = lax.broadcasted_iota(jnp.int32, (1, 8 * freqs), 1)
    came = jnp.zeros_like(arrival)
    for place, chip in enumerate(order):
        came = jnp.where(arrival >> 4 == place, chip, came)
    origin = ((zpos + chips - came) & (chips - 1)) * 2 + ((arrival >> 3) & 1)
    key_in = origin * 8 + (arrival & 7)
    place = lax.broadcasted_iota(jnp.int32, (8 * freqs, 1), 0)
    trace_index = place & (BS - 1)
    key_out = (
        (trace_index >> 1) * 8
        + ((place >> 7) & 1) * 4
        + ((place >> 8) & 1) * 2
        + (trace_index & 1)
    )
    gather[...] = jnp.where(key_in == key_out, 1.0, 0.0).astype(jnp.bfloat16)

    def sent(batch):
        low, high = batches[batch]
        span = recv.at[pl.ds(2 * low, 2 * (high - low) - (low <= home < high))]
        remote(span, span, send_sem.at[batch], recv_sem.at[batch], prv_id).wait_send()

    def relay(batch):
        low, high = batches[batch]
        mine = low <= home < high
        low, high = 2 * low, 2 * high
        arrived = recv.at[pl.ds(low, high - low - mine)]
        remote(arrived, arrived, send_sem.at[batch], recv_sem.at[batch], prv_id).wait_recv()
        if mine:
            own_copy.wait()
        span = pl.ds(low, high - low)
        down = remote(
            recv.at[span, pl.ds(0, 2)], border.at[1, span], fsend_sem.at[1], frecv_sem.at[1], prv_id
        )
        up = remote(
            recv.at[span, pl.ds(1, 2)], border.at[0, span], fsend_sem.at[0], frecv_sem.at[0], nxt_id
        )
        pl.when(has_prv)(down.start)
        pl.when(has_nxt)(up.start)

    def announce():
        for way in (1, chips - 1):
            pl.semaphore_signal(
                ready_sem,
                inc=1,
                device_id={"freq": 2 * ((zpos + way * further) % chips) + core},
                device_id_type=MESH,
            )

    for side, there in enumerate((has_prv, has_nxt)):

        @pl.when(jnp.logical_not(there))
        def _(side=side):
            border[side] = jnp.zeros(border.shape[1:], border.dtype)
            border_meta[side] = jnp.full(border_meta.shape[1:], -1.0, border_meta.dtype)

    pl.semaphore_wait(barrier, 4 * near + 3)
    own_copy = pltpu.make_async_copy(sendbuf.at[me], recv.at[2 * home + core], own_sem)
    own_copy.start()
    announce()
    meta_copies = [
        remote(meta_ref, border_meta.at[0], msend_sem.at[0], mrecv_sem.at[0], nxt_id),
        remote(meta_ref, border_meta.at[1], msend_sem.at[1], mrecv_sem.at[1], prv_id),
    ]
    pl.when(has_nxt)(meta_copies[0].start)
    pl.when(has_prv)(meta_copies[1].start)
    for kind, value in plan:
        if kind == "send":
            for place in range(*batches[value]):
                send(place)
        elif kind == "relay":
            relay(value)
        elif kind == "sent":
            sent(value)
        else:
            pl.semaphore_wait(ready_sem, 2)

    def rows_of(part):
        return part.astype(jnp.float32).reshape(8 * freqs, BS).astype(jnp.bfloat16)

    def place_band(row, block, offsets):
        for shift in range(3):
            parts = []
            for part in range(2):
                total = None
                for slot in range(SLOTS):
                    first = slot * PAIR + part * BS
                    live = jnp.where(offsets[slot] == float(shift), block[first : first + BS], 0.0)
                    total = live if total is None else total + live
                parts.append(total)
            bands[row, shift, :BS, :BS] = parts[0].astype(jnp.bfloat16)
            bands[row, shift, :BS, BS:] = parts[1].astype(jnp.bfloat16)
            bands[row, shift, BS:, :BS] = (-parts[1]).astype(jnp.bfloat16)
            bands[row, shift, BS:, BS:] = parts[0].astype(jnp.bfloat16)

    def assemble(rows, offsets, first):
        joined = jnp.concatenate([rows_of(row) for row in rows], axis=1)
        blocks = jnp.dot(gather[...], joined, preferred_element_type=jnp.float32)
        for n in range(len(rows)):
            place_band(first + n, blocks[:, n * BS : (n + 1) * BS], offsets[n])

    scale = (3.0 * BS) ** (-0.5)

    def band_term(row, source, inner):
        return jnp.dot(
            bands[row, source, :BS, :], bands[row + source - 1, inner],
            preferred_element_type=jnp.float32,
        )

    def first_term(row, source, inner):
        return jnp.dot(
            bands[row, source, :BS, :], firsts[row + source - 2, inner],
            preferred_element_type=jnp.float32,
        )

    def keep_first(row, target, total):
        value = (total * scale).astype(jnp.bfloat16)
        firsts[row - 1, target, :BS, :] = value
        firsts[row - 1, target, BS:, :BS] = -value[:, BS:]
        firsts[row - 1, target, BS:, BS:] = value[:, :BS]

    def total_of(term, row, target, sources):
        terms = [
            term(row, source, target - source + 1)
            for source in sources
            if 0 <= target - source + 1 <= 2
        ]
        return sum(terms[1:], terms[0]) if terms else jnp.zeros((BS, PAIR), jnp.float32)

    def finish(index):
        results = [
            firsts[index + 1, target, :BS, :].astype(jnp.float32) - seconds[index, target] * scale
            for target in range(3)
        ]
        for slot in range(SLOTS):
            offset = meta_ref[pl.ds(2 * index + slot, 1), :]
            for part in range(2):
                span = slice(part * BS, (part + 1) * BS)
                chosen = [
                    jnp.where(offset == float(target), results[target][:, span], 0.0)
                    for target in range(3)
                ]
                out_ref[0, part, index, slot] = (chosen[0] + chosen[1] + chosen[2]).astype(jnp.bfloat16)

    own_offsets = [
        [meta_ref[2 * n + slot : 2 * n + slot + 1, :] for slot in range(SLOTS)] for n in range(ROWS)
    ]
    assemble([recv[:, 0], recv[:, 1]], own_offsets[:2], 2)
    assemble([recv[:, 2]], own_offsets[2:], 4)
    for target in range(3):
        keep_first(3, target, total_of(band_term, 3, target, range(3)))
        partial[0, target] = total_of(band_term, 2, target, (1, 2))
        partial[1, target] = total_of(band_term, 4, target, (0, 1))
    for target in range(3):
        seconds[0, target] = total_of(first_term, 2, target, (2,))
        seconds[1, target] = total_of(first_term, 3, target, (1,))
        seconds[2, target] = total_of(first_term, 4, target, (0,))

    for side, there in ((1, has_nxt), (0, has_prv)):

        @pl.when(there)
        def _(side=side):
            mine, whole = border_meta.at[side], border.at[side]
            remote(mine, mine, msend_sem.at[side], mrecv_sem.at[side], prv_id).wait_recv()
            remote(whole, whole, fsend_sem.at[side], frecv_sem.at[side], prv_id).wait_recv()

        lines = [2 * n + 2 - 2 * side for n in range(2)]
        offsets = [
            [border_meta[side, line + slot : line + slot + 1, :] for slot in range(SLOTS)]
            for line in lines
        ]
        assemble([border[side, :, 0], border[side, :, 1]], offsets, 5 * side)
    for side in range(2):
        outer, inner = 1 + 4 * side, 2 + 2 * side
        for target in (1 - side, 2 - side):
            keep_first(outer, target, total_of(band_term, outer, target, range(3)))
        for target in range(3):
            keep_first(
                inner, target,
                partial[side, target] + total_of(band_term, inner, target, (2 * side,)),
            )
    for side in range(2):
        inner = 2 + 2 * side
        for target in range(3):
            seconds[2 * side, target] += total_of(first_term, inner, target, (2 * side, 1))
        finish(2 * side)
    for target in range(3):
        seconds[1, target] += total_of(first_term, 3, target, (0, 2))
    finish(1)

    for batch in range(len(batches)):
        if ("sent", batch) not in plan:
            sent(batch)
    for side, there in enumerate((has_nxt, has_prv)):

        @pl.when(there)
        def _(side=side):
            whole = border.at[side]
            remote(whole, whole, fsend_sem.at[side], frecv_sem.at[side], prv_id).wait_send()
            meta_copies[side].wait_send()


def schedule(chips):
    def both(*reaches):
        return [step for reach in reaches for step in (reach, -reach)]

    groups = [both(8,7), both(6)+[0], [16]+both(15,14), both(13,12,11), both(10,9), both(5,4,3), both(2,1)]
    order = [step for group in groups for step in group]
    cuts = [sum(len(group) for group in groups[:n]) for n in range(len(groups) + 1)]
    batches = list(zip(cuts[:-1], cuts[1:]))
    hops = (8, 8)
    plan = [('send', 0), ('send', 1), ('ready', 0), ('send', 2), ('send', 3), ('relay', 0), ('relay', 1), ('send', 4), ('relay', 2), ('send', 5), ('send', 6), ('relay', 3), ('relay', 4), ('relay', 5), ('relay', 6)]
    return order, batches, plan, hops


def solution(mesh):
    freqs, srows, rcols = mesh.shape["freq"], mesh.shape["srow"], mesh.shape["rcol"]

    def per_device(data_time, block_cols, row_counts):
        samples = data_time.shape[-1]
        pairs = ROWS * SLOTS
        chips = freqs // 2
        order, batches, plan, hops = schedule(chips)
        live = jnp.arange(SLOTS, dtype=jnp.int32)[:, None] < row_counts[None, :]
        cols = jnp.where(live, block_cols.T, -1000)
        return pl.pallas_call(
            functools.partial(kernel, freqs, srows, rcols, order, batches, plan, hops),
            out_shape=jax.ShapeDtypeStruct((1, 2, ROWS, SLOTS, BS, BS), jnp.bfloat16),
            in_specs=[
                pl.BlockSpec(memory_space=pl.ANY),
                pl.BlockSpec(memory_space=pltpu.VMEM),
            ],
            out_specs=pl.BlockSpec(memory_space=pltpu.VMEM),
            scratch_shapes=[
                pltpu.VMEM((pairs, PAIR, samples), jnp.bfloat16),
                pltpu.VMEM((2 * freqs, samples), jnp.bfloat16),
                pltpu.VMEM((8, BS), jnp.float32),
                pltpu.VMEM(((freqs + 1) * ROWS * 8, BS), jnp.float32),
                pltpu.VMEM((freqs, ROWS, 8, BS), jnp.bfloat16),
                pltpu.VMEM((freqs, ROWS, 8, BS), jnp.bfloat16),
                pltpu.VMEM((2, freqs, 2, 8, BS), jnp.bfloat16),
                pltpu.VMEM((2, 8, BS), jnp.float32),
                pltpu.VMEM((8 * freqs, 8 * freqs), jnp.bfloat16),
                pltpu.VMEM((7, 3, PAIR, PAIR), jnp.bfloat16),
                pltpu.VMEM((5, 3, PAIR, PAIR), jnp.bfloat16),
                pltpu.VMEM((2, 3, BS, PAIR), jnp.float32),
                pltpu.VMEM((ROWS, 3, BS, PAIR), jnp.float32),
                pltpu.SemaphoreType.DMA((pairs,)),
                pltpu.SemaphoreType.DMA,
                pltpu.SemaphoreType.REGULAR,
                pltpu.SemaphoreType.DMA((len(batches),)),
                pltpu.SemaphoreType.DMA((len(batches),)),
                pltpu.SemaphoreType.DMA((2,)),
                pltpu.SemaphoreType.DMA((2,)),
                pltpu.SemaphoreType.DMA((2,)),
                pltpu.SemaphoreType.DMA((2,)),
            ],
            compiler_params=pltpu.CompilerParams(
                collective_id=0, has_side_effects=True, vmem_limit_bytes=55574528
            ),
        )(
            data_time.reshape(pairs, PAIR, samples),
            cols,
        )

    return jax.shard_map(
        per_device,
        mesh=mesh,
        in_specs=(
            P(("srow", "rcol"), None, "freq", None, None),
            P(("srow", "rcol"), None),
            P(("srow", "rcol")),
        ),
        out_specs=P("freq", None, ("srow", "rcol"), None, None, None),
        check_vma=False,
    )
```

time: 74.6 us -> 68.2 us (0.914)
  Pallas kernels: 72.7 us -> 66.2 us
  local copies, waits for them, and re-layouts: 1.77 us -> 0.75 us
    pallas_call x1, Pallas kernels: 72.7 us -> 66.2 us  [per_device(): pl.pallas_call(functools.partial(kernel, freqs, srows, rcols, order, batc...]
    unnamed x1, local copies, waits for them, and re-layouts: 1.77 us -> 0.75 us
where the time goes in v3:
time: 68.2 us; the launch traced here: 67.7 us
  Pallas kernels  66.2 us (97%)
  local copies, waits for them, and re-layouts  0.75 us (1%)
    pallas_call x1, Pallas kernels, per_device(): pl.pallas_call(functools.partial(kernel, freqs, srows, rcols, order, batc...  66.2 us

profile of v3, /device:TPU:1, one launch (start us, length us, event | category | flops | bytes accessed | tf_op | source)
XLA Modules:
  0.0 67.7 jit_solution(5990102091836801777)
XLA Ops:
  0.0 0.7 %compare_select_fusion.cols_ref = s32[2,3]{1,0:T(2,128)S(1)} fusion(s32[3,2]{0,1:T(2,128)} %param.4, s32[3]{0:T(128)} %param.5), kind=kLoop, calls=%fused_computation | loop fusion | flops 12 | bytes 60 | tf_op jit(solution)/shard_map/jit(_where)/select_n | solution.py:333
  0.7 66.2 %shard_map.37 = bf16[1,2,3,2,128,128]{5,4,3,2,1,0:T(8,128)(2,1)S(1)} custom-call(bf16[6,256,1024]{2,1,0:T(8,128)(2,1)} %bitcast.3, s32[2,3]{1,0:T(2,128)S(1)} %compare_select_fusion.cols_ref), custom_call_target="tpu_custom_call" | custom-call | tf_op jit(solution)/shard_map/pallas_call | solution.py:334
  66.9 0.7 %copy.5 = bf16[1,2,3,2,128,128]{5,4,3,2,1,0:T(8,128)(2,1)} copy(bf16[1,2,3,2,128,128]{5,4,3,2,1,0:T(8,128)(2,1)S(1)} %shard_map.37) | data formatting | bytes 786432

commit v4 on v3

--- a/solution.py
+++ b/solution.py
@@ -31,9 +31,9 @@
 
 def kernel(
     freqs, srows, rcols, order, batches, plan, hops,
-    x_hbm, cols_ref, out_ref,
-    xv, tv, meta_ref, spread, sendbuf, recv, border, border_meta, gather, bands, firsts, partial, seconds,
-    load_sem, own_sem, ready_sem, send_sem, recv_sem, fsend_sem, frecv_sem, msend_sem, mrecv_sem,
+    x_hbm, cols_hbm, counts_hbm, out_ref,
+    xv, tv, cols_ref, counts_ref, meta_ref, spread, sendbuf, recv, border, border_meta, gather, bands, firsts, partial, seconds,
+    load_sem, index_sem, own_sem, ready_sem, send_sem, recv_sem, fsend_sem, frecv_sem, msend_sem, mrecv_sem,
 ):
     chips = freqs // 2
     me = lax.axis_index("freq")
@@ -48,7 +48,11 @@
     home = order.index(0)
 
     loads = [pltpu.make_async_copy(x_hbm.at[n], xv.at[n], load_sem.at[n]) for n in range(pairs)]
-    for load in loads:
+    index_copies = [
+        pltpu.make_async_copy(cols_hbm, cols_ref, index_sem.at[0]),
+        pltpu.make_async_copy(counts_hbm, counts_ref, index_sem.at[1]),
+    ]
+    for load in loads + index_copies:
         load.start()
 
     near, further = hops
@@ -82,9 +86,12 @@
                 ]
     sendbuf[...] = spread[: freqs * ROWS * 8, :].reshape(freqs, ROWS, 8, BS).astype(jnp.bfloat16)
 
+    for copy in index_copies:
+        copy.wait()
     for row in range(ROWS):
         for slot in range(SLOTS):
             offset = cols_ref[slot : slot + 1, row : row + 1] - (ROWS * grow + row) + 1
+            offset = jnp.where(counts_ref[:, row : row + 1] > slot, offset, -1)
             meta_ref[2 * row + slot : 2 * row + slot + 1, :] = jnp.broadcast_to(
                 offset.astype(jnp.float32), (1, BS)
             )
@@ -97,7 +104,7 @@
         )
 
     def send(place):
-        chip = (zpos + chips + order[place]) % chips
+        chip = (zpos + chips + (1 - 2 * core) * order[place]) % chips
         batch = [low <= place < high for low, high in batches].index(True)
         for other in range(2):
             target = 2 * chip + (other if order[place] else 1 - core)
@@ -111,7 +118,8 @@
     came = jnp.zeros_like(arrival)
     for place, chip in enumerate(order):
         came = jnp.where(arrival >> 4 == place, chip, came)
-    origin = ((zpos + chips - came) & (chips - 1)) * 2 + ((arrival >> 3) & 1)
+    from_core = (arrival >> 3) & 1
+    origin = ((zpos + chips - (1 - 2 * from_core) * came) & (chips - 1)) * 2 + from_core
     key_in = origin * 8 + (arrival & 7)
     place = lax.broadcasted_iota(jnp.int32, (8 * freqs, 1), 0)
     trace_index = place & (BS - 1)
@@ -143,8 +151,8 @@
         up = remote(
             recv.at[span, pl.ds(1, 2)], border.at[0, span], fsend_sem.at[0], frecv_sem.at[0], nxt_id
         )
+        pl.when(has_nxt)(up.start)
         pl.when(has_prv)(down.start)
-        pl.when(has_nxt)(up.start)
 
     def announce():
         for way in (1, chips - 1):
@@ -312,12 +320,12 @@
     def both(*reaches):
         return [step for reach in reaches for step in (reach, -reach)]
 
-    groups = [both(8,7), both(6)+[0], [16]+both(15,14), both(13,12,11), both(10,9), both(5,4,3), both(2,1)]
+    groups = [both(8,7), both(6)+[0], [16]+both(15,14), both(13,12,11), both(10,9), both(5,4), both(3,2,1)]
     order = [step for group in groups for step in group]
     cuts = [sum(len(group) for group in groups[:n]) for n in range(len(groups) + 1)]
     batches = list(zip(cuts[:-1], cuts[1:]))
     hops = (8, 8)
-    plan = [('send', 0), ('send', 1), ('ready', 0), ('send', 2), ('send', 3), ('relay', 0), ('relay', 1), ('send', 4), ('relay', 2), ('send', 5), ('send', 6), ('relay', 3), ('relay', 4), ('relay', 5), ('relay', 6)]
+    plan = [('send', 0), ('send', 1), ('ready', 0), ('send', 2), ('send', 3), ('send', 4), ('relay', 0), ('relay', 1), ('relay', 2), ('send', 5), ('send', 6), ('relay', 3), ('relay', 4), ('relay', 5), ('relay', 6)]
     return order, batches, plan, hops
 
 
@@ -329,19 +337,20 @@
         pairs = ROWS * SLOTS
         chips = freqs // 2
         order, batches, plan, hops = schedule(chips)
-        live = jnp.arange(SLOTS, dtype=jnp.int32)[:, None] < row_counts[None, :]
-        cols = jnp.where(live, block_cols.T, -1000)
         return pl.pallas_call(
             functools.partial(kernel, freqs, srows, rcols, order, batches, plan, hops),
             out_shape=jax.ShapeDtypeStruct((1, 2, ROWS, SLOTS, BS, BS), jnp.bfloat16),
             in_specs=[
                 pl.BlockSpec(memory_space=pl.ANY),
-                pl.BlockSpec(memory_space=pltpu.VMEM),
+                pl.BlockSpec(memory_space=pl.ANY),
+                pl.BlockSpec(memory_space=pl.ANY),
             ],
             out_specs=pl.BlockSpec(memory_space=pltpu.VMEM),
             scratch_shapes=[
                 pltpu.VMEM((pairs, PAIR, samples), jnp.bfloat16),
                 pltpu.VMEM((2 * freqs, samples), jnp.bfloat16),
+                pltpu.VMEM((SLOTS, ROWS), jnp.int32),
+                pltpu.VMEM((1, ROWS), jnp.int32),
                 pltpu.VMEM((8, BS), jnp.float32),
                 pltpu.VMEM(((freqs + 1) * ROWS * 8, BS), jnp.float32),
                 pltpu.VMEM((freqs, ROWS, 8, BS), jnp.bfloat16),
@@ -354,6 +363,7 @@
                 pltpu.VMEM((2, 3, BS, PAIR), jnp.float32),
                 pltpu.VMEM((ROWS, 3, BS, PAIR), jnp.float32),
                 pltpu.SemaphoreType.DMA((pairs,)),
+                pltpu.SemaphoreType.DMA((2,)),
                 pltpu.SemaphoreType.DMA,
                 pltpu.SemaphoreType.REGULAR,
                 pltpu.SemaphoreType.DMA((len(batches),)),
@@ -364,11 +374,17 @@
                 pltpu.SemaphoreType.DMA((2,)),
             ],
             compiler_params=pltpu.CompilerParams(
-                collective_id=0, has_side_effects=True, vmem_limit_bytes=55574528
+                collective_id=0, has_side_effects=True, vmem_limit_bytes=40 * 1024 * 1024
             ),
         )(
-            data_time.reshape(pairs, PAIR, samples),
-            cols,
+            *(
+                pltpu.with_memory_space_constraint(value, pltpu.HBM)
+                for value in (
+                    data_time.reshape(pairs, PAIR, samples),
+                    block_cols.T,
+                    row_counts.reshape(1, ROWS),
+                )
+            )
         )
 
     return jax.shard_map(

time: 68.2 us -> 67.1 us (0.984)
    select_n x1 -> x0, other arithmetic: 0.68 us -> none  [per_device(): cols = jnp.where(live, block_cols.T, -1000)]
where the time goes in v4:
time: 67.1 us; the launch traced here: 66.8 us
  Pallas kernels  66 us (98%)
  local copies, waits for them, and re-layouts  0.75 us (1%)
    pallas_call x1, Pallas kernels, per_device(): pl.pallas_call(functools.partial(kernel, freqs, srows, rcols, order, batc...  66 us

profile of v4, /device:TPU:1, one launch (start us, length us, event | category | flops | bytes accessed | tf_op | source)
XLA Modules:
  0.0 66.8 jit_solution(2266963712796921065)
XLA Ops:
  0.0 66.0 %shard_map.37 = bf16[1,2,3,2,128,128]{5,4,3,2,1,0:T(8,128)(2,1)S(1)} custom-call(bf16[6,256,1024]{2,1,0:T(8,128)(2,1)} %bitcast.3, s32[2,3]{1,0:T(2,128)} %bitcast.4, s32[1,3]{1,0:T(1,128)} %bitcast.5), custom_call_target="tpu_custom_call" | custom-call | tf_op jit(solution)/shard_map/pallas_call | solution.py:340
  66.0 0.7 %copy.5 = bf16[1,2,3,2,128,128]{5,4,3,2,1,0:T(8,128)(2,1)} copy(bf16[1,2,3,2,128,128]{5,4,3,2,1,0:T(8,128)(2,1)S(1)} %shard_map.37) | data formatting | bytes 786432

commit v5 on v4

--- a/solution.py
+++ b/solution.py
@@ -86,6 +86,74 @@
                 ]
     sendbuf[...] = spread[: freqs * ROWS * 8, :].reshape(freqs, ROWS, 8, BS).astype(jnp.bfloat16)
 
+    def remote(src, dst, ssem, rsem, target):
+        return pltpu.make_async_remote_copy(
+            src_ref=src, dst_ref=dst, send_sem=ssem, recv_sem=rsem,
+            device_id=target, device_id_type=MESH,
+        )
+
+    def send(place):
+        chip = (zpos + chips + (1 - 2 * core) * order[place]) % chips
+        batch = [low <= place < high for low, high in batches].index(True)
+        for other in range(2):
+            target = 2 * chip + (other if order[place] else 1 - core)
+            if order[place] or other == 0:
+                remote(
+                    sendbuf.at[target], recv.at[2 * place + core], send_sem.at[batch], recv_sem.at[batch],
+                    {"freq": target},
+                ).start()
+
+    def sent(batch):
+        low, high = batches[batch]
+        span = recv.at[pl.ds(2 * low, 2 * (high - low) - (low <= home < high))]
+        remote(span, span, send_sem.at[batch], recv_sem.at[batch], prv_id).wait_send()
+
+    def relay(batch):
+        low, high = batches[batch]
+        mine = low <= home < high
+        low, high = 2 * low, 2 * high
+        arrived = recv.at[pl.ds(low, high - low - mine)]
+        remote(arrived, arrived, send_sem.at[batch], recv_sem.at[batch], prv_id).wait_recv()
+        if mine:
+            own_copy.wait()
+        span = pl.ds(low, high - low)
+        down = remote(
+            recv.at[span, pl.ds(0, 2)], border.at[1, span], fsend_sem.at[1], frecv_sem.at[1], prv_id
+        )
+        up = remote(
+            recv.at[span, pl.ds(1, 2)], border.at[0, span], fsend_sem.at[0], frecv_sem.at[0], nxt_id
+        )
+        pl.when(has_nxt)(up.start)
+        pl.when(has_prv)(down.start)
+
+    def announce():
+        for way in (1, chips - 1):
+            pl.semaphore_signal(
+                ready_sem,
+                inc=1,
+                device_id={"freq": 2 * ((zpos + way * further) % chips) + core},
+                device_id_type=MESH,
+            )
+
+    pl.semaphore_wait(barrier, 4 * near + 3)
+    own_copy = pltpu.make_async_copy(sendbuf.at[me], recv.at[2 * home + core], own_sem)
+    own_copy.start()
+    announce()
+    def follow(steps):
+        for kind, value in steps:
+            if kind == "send":
+                for place in range(*batches[value]):
+                    send(place)
+            elif kind == "relay":
+                relay(value)
+            elif kind == "sent":
+                sent(value)
+            else:
+                pl.semaphore_wait(ready_sem, 2)
+
+    cut = [kind for kind, _ in plan].index("ready")
+    follow(plan[:cut])
+
     for copy in index_copies:
         copy.wait()
     for row in range(ROWS):
@@ -97,22 +165,19 @@
             )
     meta_ref[pairs:, :] = jnp.full((8 - pairs, BS), -1.0, jnp.float32)
 
-    def remote(src, dst, ssem, rsem, target):
-        return pltpu.make_async_remote_copy(
-            src_ref=src, dst_ref=dst, send_sem=ssem, recv_sem=rsem,
-            device_id=target, device_id_type=MESH,
-        )
-
-    def send(place):
-        chip = (zpos + chips + (1 - 2 * core) * order[place]) % chips
-        batch = [low <= place < high for low, high in batches].index(True)
-        for other in range(2):
-            target = 2 * chip + (other if order[place] else 1 - core)
-            if order[place] or other == 0:
-                remote(
-                    sendbuf.at[target], recv.at[2 * place + core], send_sem.at[batch], recv_sem.at[batch],
-                    {"freq": target},
-                ).start()
+    for side, there in enumerate((has_prv, has_nxt)):
+
+        @pl.when(jnp.logical_not(there))
+        def _(side=side):
+            border[side] = jnp.zeros(border.shape[1:], border.dtype)
+            border_meta[side] = jnp.full(border_meta.shape[1:], -1.0, border_meta.dtype)
+
+    meta_copies = [
+        remote(meta_ref, border_meta.at[0], msend_sem.at[0], mrecv_sem.at[0], nxt_id),
+        remote(meta_ref, border_meta.at[1], msend_sem.at[1], mrecv_sem.at[1], prv_id),
+    ]
+    pl.when(has_nxt)(meta_copies[0].start)
+    pl.when(has_prv)(meta_copies[1].start)
 
     arrival = lax.broadcasted_iota(jnp.int32, (1, 8 * freqs), 1)
     came = jnp.zeros_like(arrival)
@@ -131,65 +196,7 @@
     )
     gather[...] = jnp.where(key_in == key_out, 1.0, 0.0).astype(jnp.bfloat16)
 
-    def sent(batch):
-        low, high = batches[batch]
-        span = recv.at[pl.ds(2 * low, 2 * (high - low) - (low <= home < high))]
-        remote(span, span, send_sem.at[batch], recv_sem.at[batch], prv_id).wait_send()
-
-    def relay(batch):
-        low, high = batches[batch]
-        mine = low <= home < high
-        low, high = 2 * low, 2 * high
-        arrived = recv.at[pl.ds(low, high - low - mine)]
-        remote(arrived, arrived, send_sem.at[batch], recv_sem.at[batch], prv_id).wait_recv()
-        if mine:
-            own_copy.wait()
-        span = pl.ds(low, high - low)
-        down = remote(
-            recv.at[span, pl.ds(0, 2)], border.at[1, span], fsend_sem.at[1], frecv_sem.at[1], prv_id
-        )
-        up = remote(
-            recv.at[span, pl.ds(1, 2)], border.at[0, span], fsend_sem.at[0], frecv_sem.at[0], nxt_id
-        )
-        pl.when(has_nxt)(up.start)
-        pl.when(has_prv)(down.start)
-
-    def announce():
-        for way in (1, chips - 1):
-            pl.semaphore_signal(
-                ready_sem,
-                inc=1,
-                device_id={"freq": 2 * ((zpos + way * further) % chips) + core},
-                device_id_type=MESH,
-            )
-
-    for side, there in enumerate((has_prv, has_nxt)):
-
-        @pl.when(jnp.logical_not(there))
-        def _(side=side):
-            border[side] = jnp.zeros(border.shape[1:], border.dtype)
-            border_meta[side] = jnp.full(border_meta.shape[1:], -1.0, border_meta.dtype)
-
-    pl.semaphore_wait(barrier, 4 * near + 3)
-    own_copy = pltpu.make_async_copy(sendbuf.at[me], recv.at[2 * home + core], own_sem)
-    own_copy.start()
-    announce()
-    meta_copies = [
-        remote(meta_ref, border_meta.at[0], msend_sem.at[0], mrecv_sem.at[0], nxt_id),
-        remote(meta_ref, border_meta.at[1], msend_sem.at[1], mrecv_sem.at[1], prv_id),
-    ]
-    pl.when(has_nxt)(meta_copies[0].start)
-    pl.when(has_prv)(meta_copies[1].start)
-    for kind, value in plan:
-        if kind == "send":
-            for place in range(*batches[value]):
-                send(place)
-        elif kind == "relay":
-            relay(value)
-        elif kind == "sent":
-            sent(value)
-        else:
-            pl.semaphore_wait(ready_sem, 2)
+    follow(plan[cut:])
 
     def rows_of(part):
         return part.astype(jnp.float32).reshape(8 * freqs, BS).astype(jnp.bfloat16)

time: 67.1 us -> 67.2 us (level)
  no operation moved by 1% of the time
where the time goes in v5:
time: 67.2 us; the launch traced here: 66.9 us
  Pallas kernels  66.2 us (99%)
  local copies, waits for them, and re-layouts  0.75 us (1%)
    pallas_call x1, Pallas kernels, per_device(): pl.pallas_call(functools.partial(kernel, freqs, srows, rcols, order, batc...  66.2 us

profile of v5, /device:TPU:1, one launch (start us, length us, event | category | flops | bytes accessed | tf_op | source)
XLA Modules:
  0.0 66.9 jit_solution(15446821788696077750)
XLA Ops:
  0.0 66.2 %shard_map.37 = bf16[1,2,3,2,128,128]{5,4,3,2,1,0:T(8,128)(2,1)S(1)} custom-call(bf16[6,256,1024]{2,1,0:T(8,128)(2,1)} %bitcast.3, s32[2,3]{1,0:T(2,128)} %bitcast.4, s32[1,3]{1,0:T(1,128)} %bitcast.5), custom_call_target="tpu_custom_call" | custom-call | tf_op jit(solution)/shard_map/pallas_call | solution.py:347
  66.2 0.7 %copy.5 = bf16[1,2,3,2,128,128]{5,4,3,2,1,0:T(8,128)(2,1)} copy(bf16[1,2,3,2,128,128]{5,4,3,2,1,0:T(8,128)(2,1)S(1)} %shard_map.37) | data formatting | bytes 786432
